TPU v7x, 256 devices: a whole 4x4x8 slice. The times are simulated.
256 devices in a mesh: rows: 32 (over x, z), cols: 8 (over y, core).
Axes of the slice: x: 4, y: 4, z: 8, core: 2. Of those that a mesh axis runs over, the one named last changes fastest.
Arguments:
- cost: bfloat16 [32768, 8192], P('rows', 'cols'), may hold values from -12 to 12.45
- src_label: int32 [32768], P('rows'), may hold values from 0 to 63
- tgt_label: int32 [8192], P('cols'), may hold values from 0 to 63
- class_mask: int32 [64, 64], replicated, may hold values from 0 to 1, as said below
- g_start: float32 [8192], P('cols'), may hold values from -1.5 to 1.5
- f_bar: float32 [32768], P('rows'), may hold values from -6 to 6
- g_bar: float32 [8192], P('cols'), may hold values from -6 to 6
- src_emb: bfloat16 [32768, 1024], P('rows'), may hold values from -6 to 6
- tgt_emb: bfloat16 [8192, 1024], P('cols'), may hold values from -6 to 6
Outputs:
- g_start_bar: float32 [8192], P('cols')
- grad_x: float32 [1024, 32768], P('cols', 'rows')
- grad_y: float32 [1024, 8192], P('rows', 'cols')
Inputs may be any that keep to these rules, and one draw needn't show every extreme that they name: Every class may be matched with itself: class_mask[c, c] = 1; other entries are 0 or 1.
All inputs are finite; a program needn't handle non-finite values.
Results may differ from a plain program's by a relative error of at most 0.003.
Values sent between devices are 32-bit elements; how exact they have to be, the bound alone decides.
No kernel may reach another device: no remote copies, remote signals or barrier semaphores. Data moves between devices by JAX's collectives and lax.ppermute only.
A program may use at most 64 MiB of HBM per device.

v0:
```python
import math

import jax
import jax.numpy as jnp
from jax import lax
from jax.sharding import PartitionSpec as P

K = 3


EPSILON = 0.05
PENALTY = 1.0


def body(cost, src_label, tgt_label, class_mask, g_start, f_bar, g_bar, src_emb, tgt_emb):
    row_count = lax.axis_size("rows")
    col_count = lax.axis_size("cols")
    src_rows, tgt_cols = cost.shape
    width = src_emb.shape[1]
    log_source = -math.log(src_rows * row_count)
    log_target = -math.log(tgt_cols * col_count)
    class_ids = jnp.arange(class_mask.shape[0], dtype=jnp.int32)
    src_hot = (src_label[:, None] == class_ids[None, :]).astype(jnp.bfloat16)
    tgt_hot = (tgt_label[:, None] == class_ids[None, :]).astype(jnp.bfloat16)
    src_allowed = jnp.dot(
        src_hot, class_mask.astype(jnp.bfloat16), preferred_element_type=jnp.float32
    ).astype(jnp.bfloat16)
    allowed = lax.dot_general(
        src_allowed, tgt_hot, (((1,), (1,)), ((), ())), preferred_element_type=jnp.float32
    )
    shifted = cost.astype(jnp.float32) + PENALTY * (1.0 - allowed)
    col_duals = [g_start]
    row_duals = []
    for section in range(K):
        row_scores = (col_duals[-1][None, :] - shifted) / EPSILON
        row_highest = lax.pmax(jnp.max(row_scores, axis=1), "cols")
        row_summed = lax.psum(jnp.sum(jnp.exp(row_scores - row_highest[:, None]), axis=1), "cols")
        row_duals.append(EPSILON * log_source - EPSILON * (row_highest + jnp.log(row_summed)))
        scores = (row_duals[-1][:, None] - shifted) / EPSILON
        highest = lax.pmax(jnp.max(scores, axis=0), "rows")
        summed = lax.psum(jnp.sum(jnp.exp(scores - highest[None, :]), axis=0), "rows")
        col_duals.append(EPSILON * log_target - EPSILON * (highest + jnp.log(summed)))
    cost_grad = jnp.zeros_like(shifted)
    col_grad = g_bar
    for section in reversed(range(K)):
        row_now = row_duals[section]
        outer = f_bar if section == K - 1 else jnp.zeros_like(f_bar)
        plan_q = jnp.exp(
            (row_now[:, None] + col_duals[section + 1][None, :] - shifted) / EPSILON - log_target
        )
        partial_value = jnp.sum(plan_q * col_grad[None, :], axis=1)
        row_grad = outer - lax.psum(partial_value, "cols")
        plan_r = jnp.exp(
            (row_now[:, None] + col_duals[section][None, :] - shifted) / EPSILON - log_source
        )
        next_grad = -lax.psum(jnp.sum(plan_r * row_grad[:, None], axis=0), "rows")
        cost_grad = cost_grad + plan_q * col_grad[None, :] + plan_r * row_grad[:, None]
        col_grad = next_grad
    rounded = cost_grad.astype(jnp.bfloat16)
    grad_x = lax.psum_scatter(
        -lax.dot_general(
            tgt_emb, rounded, (((0,), (1,)), ((), ())), preferred_element_type=jnp.float32
        ),
        "cols",
        scatter_dimension=0,
        tiled=True,
    )
    owned_rows = width // row_count
    summed_y = lax.psum(
        -lax.dot_general(
            src_emb, rounded, (((0,), (0,)), ((), ())), preferred_element_type=jnp.float32
        ),
        "rows",
    )
    grad_y = lax.dynamic_slice_in_dim(summed_y, lax.axis_index("rows") * owned_rows, owned_rows, 0)
    return (col_grad, grad_x, grad_y)


def solution(mesh):
    placed = (
        P("rows", "cols"),
        P("rows"),
        P("cols"),
        P(),
        P("cols"),
        P("rows"),
        P("cols"),
        P("rows", None),
        P("cols", None),
    )
    return jax.shard_map(
        body,
        mesh=mesh,
        in_specs=placed,
        out_specs=(P("cols"), P("cols", "rows"), P("rows", "cols")),
        check_vma=False,
    )
```

profile of v0, /device:TPU:8, one launch (start us, length us, event | category | flops | bytes accessed | tf_op | source)
XLA Modules:
  0.0 932.4 jit_solution(15561345651326225884)
XLA Ops:
  8.0 0.0 copy-start
  8.0 0.0 copy-start.1
  8.0 0.0 all-reduce.2.cloned.1.call-start
  8.1 5.0 fusion
  13.0 11.8 %pmax.42 = f32[1024]{0:T(1024)S(1)} all-reduce(f32[1024]{0:T(1024)S(1)} %get-tuple-element.8), channel_id=1, replica_groups=mesh['rows'=32,'cols'=8] {'cols'}, use_global_device_ids=true, to_apply=%region_1.0 | all-reduce | flops 1024 | bytes 8192 | tf_op jit(solution)/shard_map/pmax | solution.py:36
  24.9 0.0 copy-done.1
  24.9 3.2 exponential_reduce_fusion.5
  28.0 12.4 %psum.91 = f32[1024]{0:T(1024)S(1)} all-reduce(f32[1024]{0:T(1024)S(1)} %exponential_reduce_fusion.5), channel_id=1, replica_groups=mesh['rows'=32,'cols'=8] {'cols'}, use_global_device_ids=true, to_apply=%region_3.0 | all-reduce | flops 1024 | bytes 8192 | tf_op jit(solution)/shard_map/psum | solution.py:37
  40.5 2.7 fusion.1
  43.1 77.7 %pmax.43 = f32[1024]{0:T(1024)S(1)} all-reduce(f32[1024]{0:T(1024)S(1)} %fusion.1), channel_id=1, replica_groups=mesh['rows'=32,'cols'=8] {'rows'}, use_global_device_ids=true, to_apply=%region_5.0 | all-reduce | flops 1024 | bytes 8192 | tf_op jit(solution)/shard_map/pmax | solution.py:40
  120.8 3.1 exponential_reduce_fusion.4
  123.9 69.6 %psum.92 = f32[1024]{0:T(1024)S(1)} all-reduce(f32[1024]{0:T(1024)S(1)} %exponential_reduce_fusion.4), channel_id=1, replica_groups=mesh['rows'=32,'cols'=8] {'rows'}, use_global_device_ids=true, to_apply=%region_7.0 | all-reduce | flops 1024 | bytes 8192 | tf_op jit(solution)/shard_map/psum | solution.py:41
  193.6 2.7 fusion.2
  196.2 12.4 %pmax.44 = f32[1024]{0:T(1024)S(1)} all-reduce(f32[1024]{0:T(1024)S(1)} %fusion.2), channel_id=1, replica_groups=mesh['rows'=32,'cols'=8] {'cols'}, use_global_device_ids=true, to_apply=%region_9.0 | all-reduce | flops 1024 | bytes 8192 | tf_op jit(solution)/shard_map/pmax | solution.py:36
  208.7 3.2 exponential_reduce_fusion.3
  211.8 12.9 %psum.93 = f32[1024]{0:T(1024)S(1)} all-reduce(f32[1024]{0:T(1024)S(1)} %exponential_reduce_fusion.3), channel_id=1, replica_groups=mesh['rows'=32,'cols'=8] {'cols'}, use_global_device_ids=true, to_apply=%region_11.0 | all-reduce | flops 1024 | bytes 8192 | tf_op jit(solution)/shard_map/psum | solution.py:37
  224.8 2.7 fusion.3
  227.4 71.7 %pmax.45 = f32[1024]{0:T(1024)S(1)} all-reduce(f32[1024]{0:T(1024)S(1)} %fusion.3), channel_id=1, replica_groups=mesh['rows'=32,'cols'=8] {'rows'}, use_global_device_ids=true, to_apply=%region_13.0 | all-reduce | flops 1024 | bytes 8192 | tf_op jit(solution)/shard_map/pmax | solution.py:40
  299.1 3.1 exponential_reduce_fusion.2
  302.2 69.6 %psum.94 = f32[1024]{0:T(1024)S(1)} all-reduce(f32[1024]{0:T(1024)S(1)} %exponential_reduce_fusion.2), channel_id=1, replica_groups=mesh['rows'=32,'cols'=8] {'rows'}, use_global_device_ids=true, to_apply=%region_15.0 | all-reduce | flops 1024 | bytes 8192 | tf_op jit(solution)/shard_map/psum | solution.py:41
  371.8 2.7 fusion.4
  374.5 11.9 %pmax.46 = f32[1024]{0:T(1024)S(1)} all-reduce(f32[1024]{0:T(1024)S(1)} %fusion.4), channel_id=1, replica_groups=mesh['rows'=32,'cols'=8] {'cols'}, use_global_device_ids=true, to_apply=%region_17.0 | all-reduce | flops 1024 | bytes 8192 | tf_op jit(solution)/shard_map/pmax | solution.py:36
  386.4 3.2 exponential_reduce_fusion.1
  389.6 12.9 %psum.95 = f32[1024]{0:T(1024)S(1)} all-reduce(f32[1024]{0:T(1024)S(1)} %exponential_reduce_fusion.1), channel_id=1, replica_groups=mesh['rows'=32,'cols'=8] {'cols'}, use_global_device_ids=true, to_apply=%region_19.0 | all-reduce | flops 1024 | bytes 8192 | tf_op jit(solution)/shard_map/psum | solution.py:37
  402.5 0.0 copy-start.3
  402.5 2.7 fusion.5
  405.2 71.7 %pmax.47 = f32[1024]{0:T(1024)S(1)} all-reduce(f32[1024]{0:T(1024)S(1)} %fusion.5), channel_id=1, replica_groups=mesh['rows'=32,'cols'=8] {'rows'}, use_global_device_ids=true, to_apply=%region_21.0 | all-reduce | flops 1024 | bytes 8192 | tf_op jit(solution)/shard_map/pmax | solution.py:40
  476.9 0.0 copy-start.2
  476.9 3.1 exponential_reduce_fusion
  480.0 69.8 %psum.96 = f32[1024]{0:T(1024)S(1)} all-reduce(f32[1024]{0:T(1024)S(1)} %exponential_reduce_fusion), channel_id=1, replica_groups=mesh['rows'=32,'cols'=8] {'rows'}, use_global_device_ids=true, to_apply=%region_23.0 | all-reduce | flops 1024 | bytes 8192 | tf_op jit(solution)/shard_map/psum | solution.py:41
  549.8 0.0 copy-done.3
  549.8 3.5 fusion.11
  553.4 11.9 %psum.97 = f32[1024]{0:T(1024)S(1)} all-reduce(f32[1024]{0:T(1024)S(1)} %fusion.11), channel_id=1, replica_groups=mesh['rows'=32,'cols'=8] {'cols'}, use_global_device_ids=true, to_apply=%region_25.0 | all-reduce | flops 1024 | bytes 8192 | tf_op jit(solution)/shard_map/psum | solution.py:52
  565.3 0.0 copy-done.2
  565.3 3.0 fusion.10
  568.3 71.6 %psum.98 = f32[1024]{0:T(1024)S(1)} all-reduce(f32[1024]{0:T(1024)S(1)} %fusion.10), channel_id=1, replica_groups=mesh['rows'=32,'cols'=8] {'rows'}, use_global_device_ids=true, to_apply=%region_27.0 | all-reduce | flops 1024 | bytes 8192 | tf_op jit(solution)/shard_map/psum | solution.py:56
  639.9 3.5 fusion.9
  643.5 12.4 %psum.99 = f32[1024]{0:T(1024)S(1)} all-reduce(f32[1024]{0:T(1024)S(1)} %fusion.9), channel_id=1, replica_groups=mesh['rows'=32,'cols'=8] {'cols'}, use_global_device_ids=true, to_apply=%region_29.0 | all-reduce | flops 1024 | bytes 8192 | tf_op jit(solution)/shard_map/psum | solution.py:52
  655.9 3.0 fusion.8
  658.9 69.6 %psum.100 = f32[1024]{0:T(1024)S(1)} all-reduce(f32[1024]{0:T(1024)S(1)} %fusion.8), channel_id=1, replica_groups=mesh['rows'=32,'cols'=8] {'rows'}, use_global_device_ids=true, to_apply=%region_31.0 | all-reduce | flops 1024 | bytes 8192 | tf_op jit(solution)/shard_map/psum | solution.py:56
  728.6 3.5 fusion.7
  732.1 12.4 %psum.101 = f32[1024]{0:T(1024)S(1)} all-reduce(f32[1024]{0:T(1024)S(1)} %fusion.7), channel_id=1, replica_groups=mesh['rows'=32,'cols'=8] {'cols'}, use_global_device_ids=true, to_apply=%region_33.0 | all-reduce | flops 1024 | bytes 8192 | tf_op jit(solution)/shard_map/psum | solution.py:52
  744.5 10.5 %add_convert_fusion = (bf16[1024,1024]{1,0:T(8,128)(2,1)S(1)}, f32[1024]{0:T(1024)S(1)}) fusion(f32[1024,1024]{1,0:T(8,128)} %get-tuple-element.9, f32[1024]{0:T(1024)S(1)} %broadcast_subtract_fusion, f32[1024]{0:T(1024)S(1)} %neg.22, f32[1024]{0:T(1024)S(1)} %broadcast_subtract_fusion.1, f32[1024]{0:T(1024)S(1)} %neg.21, f32[1024]{0:T(1024)S(1)} %sub.194, ...), kind=kLoop, calls=%fused_computation.2 | loop fusion | flops 38796288 | bytes 6348800 | tf_op jit(solution)/shard_map/convert_element_type | solution.py:59
  755.1 0.0 copy-start.4
  755.1 1.4 copy-done.4
  756.5 0.0 copy-done
  756.5 4.4 negate_bitcast_fusion
  760.9 0.0 all-reduce.2.cloned.1.call-update
  760.9 0.0 reduce-scatter.2.cloned.1.call-start
  760.9 6.5 negate_bitcast_fusion.1
  767.5 0.0 reduce-scatter.2.cloned.1.call-update
  767.5 72.0 %psum.102 = f32[1024]{0:T(1024)S(1)} all-reduce(f32[1024]{0:T(1024)S(1)} %get-tuple-element.7), channel_id=1, replica_groups=mesh['rows'=32,'cols'=8] {'rows'}, use_global_device_ids=true, to_apply=%region_35.0 | all-reduce | flops 1024 | bytes 8192 | tf_op jit(solution)/shard_map/psum | solution.py:56
  839.4 0.6 neg.23
  840.0 80.8 %all-reduce.2.cloned.1.call-done = f32[1024,1024]{0,1:T(8,128)} async-done(((f32[1024,1024]{0,1:T(8,128)}), f32[1024,1024]{0,1:T(8,128)}) %all-reduce.2.cloned.1.call-update) | async-done | bytes 4194320 | tf_op jit(solution)/shard_map/psum | solution.py:69
  920.8 1.2 constant_dynamic-slice_fusion
  922.1 0.8 copy.13
  922.9 0.0 reduce-scatter.2.cloned.1.call-done
  922.9 2.0 copy.12
  (11 shorter events, 0.1 us)
Async XLA Ops:
  8.0 748.5 %copy-start = (bf16[1024,1024]{1,0:T(8,128)(2,1)S(1)}, bf16[1024,1024]{1,0:T(8,128)(2,1)}, u32[]{:S(2)}) copy-start(bf16[1024,1024]{1,0:T(8,128)(2,1)} %param.16) | copy-start | bytes 6291460
  8.0 16.8 %copy-start.1 = (f32[1024]{0:T(1024)S(1)}, f32[1024]{0:T(1024)}, u32[]{:S(2)}) copy-start(f32[1024]{0:T(1024)} %param.13) | copy-start | bytes 12292
  8.0 912.8 %all-reduce.2.cloned.1.call-start = ((), (), s32[]{:S(2)}) async-start(), calls=%async_computation.2 | async-start | bytes 8388608 | tf_op jit(solution)/shard_map/psum | solution.py:69
  402.5 147.3 %copy-start.3 = (f32[1024]{0:T(1024)S(1)}, f32[1024]{0:T(1024)}, u32[]{:S(2)}) copy-start(f32[1024]{0:T(1024)} %param.15) | copy-start | bytes 12292
  476.9 88.4 %copy-start.2 = (f32[1024]{0:T(1024)S(1)}, f32[1024]{0:T(1024)}, u32[]{:S(2)}) copy-start(f32[1024]{0:T(1024)} %param.14) | copy-start | bytes 12292
  755.1 1.4 copy-start.4
  760.9 162.0 %reduce-scatter.2.cloned.1.call-start = ((), (), s32[]{:S(2)}) async-start(), calls=%async_computation.1 | async-start | bytes 4718592 | tf_op jit(solution)/shard_map/reduce_scatter | solution.py:60
Sparse Core Ops, SparseCore 0:
  761.0 159.7 all-reduce.1
Sparse Core Ops, SparseCore 1:
  767.6 33.2 reduce-scatter.1
where the time goes:
time: 933 us; the launch traced here: 932 us
  blocking collectives  754 us (81%)
  waiting for transfers between devices  80.8 us (9%)
  other arithmetic  60 us (6%)
  matrix products  15.9 us (2%)
  between operations  15.7 us (2%)
    pmax x3, blocking collectives, body(): highest = lax.pmax(jnp.max(scores, axis=0), 'rows')  221 us
    psum x3, blocking collectives, body(): next_grad = -lax.psum(jnp.sum(plan_r * row_grad[:, None], axis=0), 'rows')  213 us
    psum x3, blocking collectives, body(): lax.psum(jnp.sum(jnp.exp(scores - highest[None, :]), axis=0), 'rows')  209 us
    psum x1, waiting for transfers between devices, body(): lax.psum(-lax.dot_general(src_emb, rounded, (((0,), (0,)), ((), ())), pre...  80.8 us
    psum x3, blocking collectives, body(): lax.psum(jnp.sum(jnp.exp(row_scores - row_highest[:, None]), axis=1), 'co...  38.3 us
    psum x3, blocking collectives, body(): row_grad = outer - lax.psum(partial_value, 'cols')  36.7 us
    pmax x3, blocking collectives, body(): row_highest = lax.pmax(jnp.max(row_scores, axis=1), 'cols')  36.1 us
  transfers between devices with their start and end apart: 2, of which 1 were waited for; matrix products, arithmetic and copies ran while one was open for 1% of the time, Pallas kernels for 0%

commit v1 on v0

--- a/solution.py
+++ b/solution.py
@@ -10,6 +10,25 @@
 
 EPSILON = 0.05
 PENALTY = 1.0
+
+
+def gathered(value, axis):
+    count = lax.axis_size(axis)
+    copies = jnp.broadcast_to(value.reshape(1, 8, -1), (count, 8, value.shape[0] // 8))
+    return lax.all_to_all(copies, axis, 0, 0, tiled=True).reshape(count, -1)
+
+
+def total(value, axis):
+    return jnp.sum(gathered(value, axis), axis=0)
+
+
+def log_total(scores, reduced, axis):
+    highest = jnp.max(scores, axis=reduced, keepdims=True)
+    summed = jnp.sum(jnp.exp(scores - highest), axis=reduced)
+    local = highest.reshape(-1) + jnp.log(summed)
+    parts = gathered(local, axis)
+    top = jnp.max(parts, axis=0)
+    return top + jnp.log(jnp.sum(jnp.exp(parts - top[None, :]), axis=0))
 
 
 def body(cost, src_label, tgt_label, class_mask, g_start, f_bar, g_bar, src_emb, tgt_emb):
@@ -33,13 +52,9 @@
     row_duals = []
     for section in range(K):
         row_scores = (col_duals[-1][None, :] - shifted) / EPSILON
-        row_highest = lax.pmax(jnp.max(row_scores, axis=1), "cols")
-        row_summed = lax.psum(jnp.sum(jnp.exp(row_scores - row_highest[:, None]), axis=1), "cols")
-        row_duals.append(EPSILON * log_source - EPSILON * (row_highest + jnp.log(row_summed)))
+        row_duals.append(EPSILON * log_source - EPSILON * log_total(row_scores, 1, "cols"))
         scores = (row_duals[-1][:, None] - shifted) / EPSILON
-        highest = lax.pmax(jnp.max(scores, axis=0), "rows")
-        summed = lax.psum(jnp.sum(jnp.exp(scores - highest[None, :]), axis=0), "rows")
-        col_duals.append(EPSILON * log_target - EPSILON * (highest + jnp.log(summed)))
+        col_duals.append(EPSILON * log_target - EPSILON * log_total(scores, 0, "rows"))
     cost_grad = jnp.zeros_like(shifted)
     col_grad = g_bar
     for section in reversed(range(K)):
@@ -49,31 +64,42 @@
             (row_now[:, None] + col_duals[section + 1][None, :] - shifted) / EPSILON - log_target
         )
         partial_value = jnp.sum(plan_q * col_grad[None, :], axis=1)
-        row_grad = outer - lax.psum(partial_value, "cols")
+        row_grad = outer - total(partial_value, "cols")
         plan_r = jnp.exp(
             (row_now[:, None] + col_duals[section][None, :] - shifted) / EPSILON - log_source
         )
-        next_grad = -lax.psum(jnp.sum(plan_r * row_grad[:, None], axis=0), "rows")
+        next_partial = jnp.sum(plan_r * row_grad[:, None], axis=0)
         cost_grad = cost_grad + plan_q * col_grad[None, :] + plan_r * row_grad[:, None]
-        col_grad = next_grad
+        if section:
+            col_grad = -total(next_partial, "rows")
     rounded = cost_grad.astype(jnp.bfloat16)
-    grad_x = lax.psum_scatter(
-        -lax.dot_general(
-            tgt_emb, rounded, (((0,), (1,)), ((), ())), preferred_element_type=jnp.float32
-        ),
-        "cols",
-        scatter_dimension=0,
-        tiled=True,
+    x_count, z_count = 4, row_count // 4
+    owned = width // row_count
+    src_ordered = src_emb.reshape(src_rows, x_count, z_count, owned).transpose(0, 2, 1, 3)
+    along_z = [[x * z_count + z for z in range(z_count)] for x in range(x_count)]
+    along_x = [[x * z_count + z for x in range(x_count)] for z in range(z_count)]
+    y_part = -lax.dot_general(
+        src_ordered.reshape(src_rows, width),
+        rounded,
+        (((0,), (0,)), ((), ())),
+        preferred_element_type=jnp.float32,
     )
-    owned_rows = width // row_count
-    summed_y = lax.psum(
-        -lax.dot_general(
-            src_emb, rounded, (((0,), (0,)), ((), ())), preferred_element_type=jnp.float32
-        ),
-        "rows",
+    y_part = lax.psum_scatter(
+        y_part, "rows", scatter_dimension=0, tiled=True, axis_index_groups=along_z
     )
-    grad_y = lax.dynamic_slice_in_dim(summed_y, lax.axis_index("rows") * owned_rows, owned_rows, 0)
-    return (col_grad, grad_x, grad_y)
+    x_part = -lax.dot_general(
+        tgt_emb, rounded, (((0,), (1,)), ((), ())), preferred_element_type=jnp.float32
+    )
+    x_blocks = lax.all_to_all(
+        x_part.reshape(col_count, width // col_count, src_rows), "cols", 0, 0, tiled=True
+    )
+    grad_x = jnp.sum(x_blocks, axis=0)
+    g_start_bar = -total(next_partial, "rows")
+    y_blocks = lax.all_to_all(
+        y_part.reshape(x_count, owned, tgt_cols), "rows", 0, 0, tiled=True, axis_index_groups=along_x
+    )
+    grad_y = jnp.sum(y_blocks, axis=0)
+    return (g_start_bar, grad_x, grad_y)
 
 
 def solution(mesh):

time: 933 us -> 292 us (0.31)
  blocking collectives: 754 us -> 117 us
  waiting for transfers between devices: 80.8 us -> 57 us
  starting transfers between devices: 0.08 us -> 16.8 us
    psum x12 -> x0, blocking collectives: 497 us -> none  [the longest x3 213 us: body(): next_grad = -lax.psum(jnp.sum(plan_r * row_grad[:, None], axis=0), 'rows')]
    pmax x6 -> x0, blocking collectives: 257 us -> none  [the longest x3 221 us: body(): highest = lax.pmax(jnp.max(scores, axis=0), 'rows')]
    all_to_all x0 -> x10, blocking collectives: none -> 117 us  [gathered(): return lax.all_to_all(copies, axis, 0, 0, tiled=True).reshape(count, -1)]
    psum x1 -> x0, waiting for transfers between devices: 80.8 us -> none  [body(): lax.psum(-lax.dot_general(src_emb, rounded, (((0,), (0,)), ((), ())), pre...]
    reduce_scatter x1, waiting for transfers between devices: 0.01 us -> 31.3 us  [body(): lax.psum_scatter(y_part, 'rows', scatter_dimension=0, tiled=True, axis_in...]
    all_to_all x0 -> x4, waiting for transfers between devices: none -> 25.7 us  [the longest x1 15 us: body(): lax.all_to_all(x_part.reshape(col_count, width // col_count, src_rows), '...]
    all_to_all x0 -> x4, starting transfers between devices: none -> 16.8 us  [the longest x2 8.57 us: gathered(): return lax.all_to_all(copies, axis, 0, 0, tiled=True).reshape(count, -1)]
    reduce_sum x8 -> x22, other arithmetic: 24.7 us -> 18.3 us  [the longest x6 7.91 us: log_total(): summed = jnp.sum(jnp.exp(scores - highest), axis=reduced)]
  transfers between devices with their start and end apart: 2 -> 5, of which waited for: 1 -> 4; matrix products, arithmetic and copies ran while one was open for 1% -> 7% of each run, Pallas kernels for 0% -> 0%
where the time goes in v1:
time: 292 us; the launch traced here: 290 us
  blocking collectives  117 us (40%)
  waiting for transfers between devices  57 us (20%)
  other arithmetic  54.6 us (19%)
  starting transfers between devices  16.8 us (6%)
  matrix products  15.4 us (5%)
  local copies, waits for them, and re-layouts  14.8 us (5%)
  between operations  14.4 us (5%)
    all_to_all x10, blocking collectives, gathered(): return lax.all_to_all(copies, axis, 0, 0, tiled=True).reshape(count, -1)  117 us
    reduce_scatter x1, waiting for transfers between devices, body(): lax.psum_scatter(y_part, 'rows', scatter_dimension=0, tiled=True, axis_in...  31.3 us
    all_to_all x1, waiting for transfers between devices, body(): lax.all_to_all(x_part.reshape(col_count, width // col_count, src_rows), '...  15 us
    reduce_max x5, other arithmetic, log_total(): highest = jnp.max(scores, axis=reduced, keepdims=True)  14.1 us
    convert_element_type x1, other arithmetic, body(): rounded = cost_grad.astype(jnp.bfloat16)  10.7 us
    reduce_sum x3, other arithmetic, body(): partial_value = jnp.sum(plan_q * col_grad[None, :], axis=1)  10.6 us
    all_to_all x2, starting transfers between devices, gathered(): return lax.all_to_all(copies, axis, 0, 0, tiled=True).reshape(count, -1)  8.57 us
    unnamed x23, local copies, waits for them, and re-layouts  8.17 us
  transfers between devices with their start and end apart: 5, of which 4 were waited for; matrix products, arithmetic and copies ran while one was open for 7% of the time, Pallas kernels for 0%

profile of v1, /device:TPU:8, one launch (start us, length us, event | category | flops | bytes accessed | tf_op | source)
XLA Modules:
  0.0 289.8 jit_solution(15045906202471241204)
XLA Ops:
  7.2 0.0 copy-start
  7.2 0.0 copy-start.7
  7.2 5.1 %fusion = (f32[1024]{0:T(1024)S(1)}, f32[1024,1024]{1,0:T(8,128)}) fusion(f32[1024]{0:T(1024)} %param.13, s32[1024]{0:T(1024)} %param.11, s32[1024]{0:T(1024)} %param.10, s32[64,64]{1,0:T(8,128)} %param.12, bf16[1024,1024]{1,0:T(8,128)(2,1)} %param.9), kind=kOutput, calls=%fused_computation.21 | convolution fusion | flops 149097472 | bytes 6324224 | tf_op jit(solution)/shard_map/dot_general | solution.py:47
  12.3 0.0 copy-done.7
  12.3 3.2 %exponential_reduce_fusion.5 = f32[1024]{0:T(1024)S(1)} fusion(f32[1024,1024]{1,0:T(8,128)} %get-tuple-element.6, f32[1024]{0:T(1024)S(1)} %get-tuple-element.5, f32[1024]{0:T(1024)S(1)} %copy-done.7), kind=kLoop, calls=%fused_computation.18 | loop fusion | flops 4193280 | bytes 4206592 | tf_op jit(solution)/shard_map/reduce_sum | solution.py:27
  15.5 8.7 %all_to_all.70 = f32[8,8,128]{2,1,0:T(8,128)S(1)} all-to-all(f32[8,8,128]{2,1,0:T(8,128)S(1)} %broadcast_in_dim.36), channel_id=1, replica_groups=mesh['rows'=32,'cols'=8] {'cols'}, dimensions={0} | all-to-all | bytes 65536 | tf_op jit(solution)/shard_map/all_to_all | solution.py:18
  24.2 2.8 fusion.1
  27.0 0.6 copy-done.1
  27.6 0.9 exponential_reduce_fusion.4
  28.6 21.4 %all_to_all.71 = f32[32,8,128]{2,1,0:T(8,128)S(1)} all-to-all(f32[32,8,128]{2,1,0:T(8,128)S(1)} %broadcast_in_dim.37), channel_id=1, replica_groups=mesh['rows'=32,'cols'=8] {'rows'}, dimensions={0} | all-to-all | bytes 262144 | tf_op jit(solution)/shard_map/all_to_all | solution.py:18
  50.0 2.8 fusion.2
  52.9 0.6 copy-done.2
  53.4 1.0 exponential_reduce_fusion.3
  54.5 7.8 %all_to_all.72 = f32[8,8,128]{2,1,0:T(8,128)S(1)} all-to-all(f32[8,8,128]{2,1,0:T(8,128)S(1)} %broadcast_in_dim.38), channel_id=1, replica_groups=mesh['rows'=32,'cols'=8] {'cols'}, dimensions={0} | all-to-all | bytes 65536 | tf_op jit(solution)/shard_map/all_to_all | solution.py:18
  62.4 2.8 fusion.3
  65.2 0.6 copy-done.3
  65.8 0.9 exponential_reduce_fusion.2
  66.7 13.9 %all_to_all.73 = f32[32,8,128]{2,1,0:T(8,128)S(1)} all-to-all(f32[32,8,128]{2,1,0:T(8,128)S(1)} %broadcast_in_dim.39), channel_id=1, replica_groups=mesh['rows'=32,'cols'=8] {'rows'}, dimensions={0} | all-to-all | bytes 262144 | tf_op jit(solution)/shard_map/all_to_all | solution.py:18
  80.7 2.8 fusion.4
  83.5 0.6 copy-done.4
  84.1 1.0 exponential_reduce_fusion.1
  85.1 7.8 %all_to_all.74 = f32[8,8,128]{2,1,0:T(8,128)S(1)} all-to-all(f32[8,8,128]{2,1,0:T(8,128)S(1)} %broadcast_in_dim.40), channel_id=1, replica_groups=mesh['rows'=32,'cols'=8] {'cols'}, dimensions={0} | all-to-all | bytes 65536 | tf_op jit(solution)/shard_map/all_to_all | solution.py:18
  93.0 0.0 copy-start.9
  93.0 2.8 fusion.5
  95.8 0.6 copy-done.5
  96.4 0.9 exponential_reduce_fusion
  97.3 13.9 %all_to_all.75 = f32[32,8,128]{2,1,0:T(8,128)S(1)} all-to-all(f32[32,8,128]{2,1,0:T(8,128)S(1)} %broadcast_in_dim.41), channel_id=1, replica_groups=mesh['rows'=32,'cols'=8] {'rows'}, dimensions={0} | all-to-all | bytes 262144 | tf_op jit(solution)/shard_map/all_to_all | solution.py:18
  111.3 0.0 copy-done.9
  111.3 3.5 %fusion.11 = f32[1024]{0:T(1024)S(1)} fusion(f32[1024,1024]{1,0:T(8,128)} %get-tuple-element.6, f32[1024]{0:T(1024)S(1)} %copy-done.9, f32[1024]{0:T(1024)S(1)} %subtract_bitcast_fusion.2, f32[1024]{0:T(1024)S(1)} %subtract_bitcast_fusion.3), kind=kLoop, calls=%fused_computation.32 | loop fusion | flops 6290432 | bytes 4210688 | tf_op jit(solution)/shard_map/reduce_sum | solution.py:66
  114.8 7.8 %all_to_all.76 = f32[8,8,128]{2,1,0:T(8,128)S(1)} all-to-all(f32[8,8,128]{2,1,0:T(8,128)S(1)} %broadcast_in_dim.43), channel_id=1, replica_groups=mesh['rows'=32,'cols'=8] {'cols'}, dimensions={0} | all-to-all | bytes 65536 | tf_op jit(solution)/shard_map/all_to_all | solution.py:18
  122.7 0.0 copy-done.8
  122.7 3.0 %fusion.10 = f32[1024]{0:T(1024)S(1)} fusion(f32[1024,1024]{1,0:T(8,128)} %get-tuple-element.6, f32[1024]{0:T(1024)S(1)} %bitcast_subtract_fusion, f32[1024]{0:T(1024)S(1)} %subtract_bitcast_fusion.3, f32[1024]{0:T(1024)S(1)} %subtract_bitcast_fusion.4), kind=kLoop, calls=%fused_computation.31 | loop fusion | flops 6290432 | bytes 4210688 | tf_op jit(solution)/shard_map/reduce_sum | solution.py:71
  125.7 13.9 %all_to_all.77 = f32[32,8,128]{2,1,0:T(8,128)S(1)} all-to-all(f32[32,8,128]{2,1,0:T(8,128)S(1)} %broadcast_in_dim.45), channel_id=1, replica_groups=mesh['rows'=32,'cols'=8] {'rows'}, dimensions={0} | all-to-all | bytes 262144 | tf_op jit(solution)/shard_map/all_to_all | solution.py:18
  139.6 3.5 %fusion.9 = f32[1024]{0:T(1024)S(1)} fusion(f32[1024,1024]{1,0:T(8,128)} %get-tuple-element.6, f32[1024]{0:T(1024)S(1)} %negate_bitcast_fusion.3, f32[1024]{0:T(1024)S(1)} %subtract_bitcast_fusion.4, f32[1024]{0:T(1024)S(1)} %subtract_bitcast_fusion.5), kind=kLoop, calls=%fused_computation.30 | loop fusion | flops 6290432 | bytes 4210688 | tf_op jit(solution)/shard_map/reduce_sum | solution.py:66
  143.2 7.8 %all_to_all.78 = f32[8,8,128]{2,1,0:T(8,128)S(1)} all-to-all(f32[8,8,128]{2,1,0:T(8,128)S(1)} %broadcast_in_dim.47), channel_id=1, replica_groups=mesh['rows'=32,'cols'=8] {'cols'}, dimensions={0} | all-to-all | bytes 65536 | tf_op jit(solution)/shard_map/all_to_all | solution.py:18
  151.0 3.0 %fusion.8 = f32[1024]{0:T(1024)S(1)} fusion(f32[1024,1024]{1,0:T(8,128)} %get-tuple-element.6, f32[1024]{0:T(1024)S(1)} %subtract_bitcast_fusion.1, f32[1024]{0:T(1024)S(1)} %subtract_bitcast_fusion.5, f32[1024]{0:T(1024)S(1)} %subtract_bitcast_fusion.6), kind=kLoop, calls=%fused_computation.29 | loop fusion | flops 6290432 | bytes 4210688 | tf_op jit(solution)/shard_map/reduce_sum | solution.py:71
  154.0 13.9 %all_to_all.79 = f32[32,8,128]{2,1,0:T(8,128)S(1)} all-to-all(f32[32,8,128]{2,1,0:T(8,128)S(1)} %broadcast_in_dim.49), channel_id=1, replica_groups=mesh['rows'=32,'cols'=8] {'rows'}, dimensions={0} | all-to-all | bytes 262144 | tf_op jit(solution)/shard_map/all_to_all | solution.py:18
  167.9 3.5 %fusion.7 = f32[1024]{0:T(1024)S(1)} fusion(f32[1024,1024]{1,0:T(8,128)} %get-tuple-element.6, f32[1024]{0:T(1024)S(1)} %negate_bitcast_fusion.2, f32[1024]{0:T(1024)S(1)} %subtract_bitcast_fusion.6, f32[1024]{0:T(1024)S(1)} %subtract_bitcast_fusion.7), kind=kLoop, calls=%fused_computation.28 | loop fusion | flops 6290432 | bytes 4210688 | tf_op jit(solution)/shard_map/reduce_sum | solution.py:66
  171.5 0.6 broadcast_in_dim.51
  172.1 4.7 %all-to-all-start.10 = ((f32[8,8,128]{2,1,0:T(8,128)}), f32[8,8,128]{2,1,0:T(8,128)S(1)}, u32[]{:S(2)}, u32[]{:S(2)}) async-start(f32[8,8,128]{2,1,0:T(8,128)} %broadcast_in_dim.51), calls=%async_computation.10 | async-start | bytes 65536 | tf_op jit(solution)/shard_map/all_to_all | solution.py:18
  176.8 0.0 reduce-scatter.2.cloned.1.call-start
  176.8 4.0 %copy.15 = bf16[1024,1024]{0,1:T(8,128)(2,1)} copy(bf16[1024,1024]{1,0:T(8,128)(2,1)} %param.16) | data formatting | bytes 4194304 | tf_op args[7]
  180.8 3.2 %copy.16 = bf16[1024,8,4,32]{0,3,2,1:T(8,128)(2,1)} copy(bf16[1024,8,4,32]{0,3,1,2:T(8,128)(2,1)} %bitcast.56) | data formatting | bytes 4194304 | tf_op jit(solution)/shard_map/transpose | solution.py:78
  184.0 0.0 all-to-all-done.10
  184.0 0.0 copy-start.6
  184.0 10.7 %add_convert_fusion = (bf16[1024,1024]{1,0:T(8,128)(2,1)S(1)}, f32[1024]{0:T(1024)S(1)}) fusion(f32[1024,1024]{1,0:T(8,128)} %get-tuple-element.6, f32[1024]{0:T(1024)S(1)} %subtract_bitcast_fusion, f32[1024]{0:T(1024)S(1)} %negate_bitcast_fusion.2, f32[1024]{0:T(1024)S(1)} %subtract_bitcast_fusion.1, f32[1024]{0:T(1024)S(1)} %negate_bitcast_fusion.3, ...), kind=kLoop, calls=%fused_computation.1 | loop fusion | flops 38796288 | bytes 6348800 | tf_op jit(solution)/shard_map/convert_element_type | solution.py:75
  194.7 1.3 copy-done.10
  196.0 0.0 copy-done.6
  196.0 4.4 %negate_bitcast_fusion = f32[1024,1024]{0,1:T(8,128)} fusion(bf16[1024,1024]{1,0:T(8,128)(2,1)S(1)} %get-tuple-element.3, bf16[1024,1024]{0,1:T(8,128)(2,1)S(1)} %bitcast.58), kind=kOutput, calls=%fused_computation | convolution fusion | flops 2148532224 | bytes 8388608 | tf_op jit(solution)/shard_map/dot_general | solution.py:81
  200.4 0.0 reduce-scatter.2.cloned.1.call-update
  200.4 0.7 broadcast_in_dim.53
  201.1 3.9 %all-to-all-start.11 = ((f32[32,8,128]{2,1,0:T(8,128)}), f32[32,8,128]{2,1,0:T(8,128)S(1)}, u32[]{:S(2)}, u32[]{:S(2)}) async-start(f32[32,8,128]{2,1,0:T(8,128)} %broadcast_in_dim.53), calls=%async_computation.11 | async-start | bytes 262144 | tf_op jit(solution)/shard_map/all_to_all | solution.py:18
  205.0 0.0 copy-done
  205.0 5.9 %convolution_negate_fusion = f32[1024,1024]{0,1:T(8,128)} fusion(bf16[1024,1024]{1,0:T(8,128)(2,1)} %copy-done.10, bf16[1024,1024]{1,0:T(8,128)(2,1)S(1)} %copy-done), kind=kOutput, calls=%fused_computation.33 | convolution fusion | flops 2148532224 | bytes 8388608 | tf_op jit(solution)/shard_map/dot_general | solution.py:90
  210.9 5.3 %all-to-all-done.11 = f32[32,8,128]{2,1,0:T(8,128)S(1)} async-done(((f32[32,8,128]{2,1,0:T(8,128)}), f32[32,8,128]{2,1,0:T(8,128)S(1)}, u32[]{:S(2)}, u32[]{:S(2)}) %all-to-all-start.11) | async-done | bytes 131104 | tf_op jit(solution)/shard_map/all_to_all | solution.py:18
  216.2 4.8 %all-to-all-start.12 = ((f32[8,128,1024]{2,1,0:T(8,128)}), f32[8,128,1024]{2,1,0:T(8,128)}, u32[]{:S(2)}, u32[]{:S(2)}) async-start(f32[8,128,1024]{2,1,0:T(8,128)} %bitcast.57), calls=%async_computation.12 | async-start | bytes 8388608 | tf_op jit(solution)/shard_map/all_to_all | solution.py:93
  221.0 31.3 %reduce-scatter.2.cloned.1.call-done = f32[128,1024]{0,1:T(8,128)} async-done(((f32[1024,1024]{0,1:T(8,128)}), f32[128,1024]{0,1:T(8,128)}) %reduce-scatter.2.cloned.1.call-update) | async-done | bytes 524304 | tf_op jit(solution)/shard_map/reduce_scatter | solution.py:87
  252.2 2.1 copy.17
  254.3 15.0 %all-to-all-done.12 = f32[8,128,1024]{2,1,0:T(8,128)} async-done(((f32[8,128,1024]{2,1,0:T(8,128)}), f32[8,128,1024]{2,1,0:T(8,128)}, u32[]{:S(2)}, u32[]{:S(2)}) %all-to-all-start.12) | async-done | bytes 4194336 | tf_op jit(solution)/shard_map/all_to_all | solution.py:93
  269.3 3.5 %all-to-all-start.13 = ((f32[4,32,1024]{2,1,0:T(8,128)}), f32[4,32,1024]{2,1,0:T(8,128)S(1)}, u32[]{:S(2)}, u32[]{:S(2)}) async-start(f32[4,32,1024]{2,1,0:T(8,128)} %bitcast.30), calls=%async_computation.14 | async-start | bytes 1048576 | tf_op jit(solution)/shard_map/all_to_all | solution.py:98
  272.8 0.6 negate_bitcast_fusion.1
  273.4 3.4 %reduce_sum.261 = f32[128,1024]{1,0:T(8,128)} reduce(f32[8,128,1024]{2,1,0:T(8,128)} %all-to-all-done.12, f32[]{:T(128)} %constant.32.clone.1), dimensions={0}, to_apply=%region_36.0 | reduce | flops 917504 | bytes 4718596 | tf_op jit(solution)/shard_map/reduce_sum | solution.py:96
  276.8 5.5 %all-to-all-done.13 = f32[4,32,1024]{2,1,0:T(8,128)S(1)} async-done(((f32[4,32,1024]{2,1,0:T(8,128)}), f32[4,32,1024]{2,1,0:T(8,128)S(1)}, u32[]{:S(2)}, u32[]{:S(2)}) %all-to-all-start.13) | async-done | bytes 524320 | tf_op jit(solution)/shard_map/all_to_all | solution.py:98
  282.3 0.7 reduce_sum.262
  (52 shorter events, 0.7 us)
Async XLA Ops:
  7.2 197.8 %copy-start = (bf16[1024,1024]{1,0:T(8,128)(2,1)S(1)}, bf16[1024,1024]{1,0:T(8,128)(2,1)}, u32[]{:S(2)}) copy-start(bf16[1024,1024]{1,0:T(8,128)(2,1)} %param.17) | copy-start | bytes 6291460
  7.2 5.1 %copy-start.7 = (f32[1024]{0:T(1024)S(1)}, f32[1024]{0:T(1024)}, u32[]{:S(2)}) copy-start(f32[1024]{0:T(1024)} %param.13) | copy-start | bytes 12292
  24.2 3.4 %copy-start.1 = (f32[1024,1024]{1,0:T(8,128)S(1)}, f32[1024,1024]{1,0:T(8,128)}, u32[]{:S(2)}) copy-start(f32[1024,1024]{1,0:T(8,128)} %get-tuple-element.6) | copy-start | bytes 12582916
  50.0 3.4 %copy-start.2 = (f32[1024,1024]{1,0:T(8,128)S(1)}, f32[1024,1024]{1,0:T(8,128)}, u32[]{:S(2)}) copy-start(f32[1024,1024]{1,0:T(8,128)} %get-tuple-element.6) | copy-start | bytes 12582916
  62.3 3.4 %copy-start.3 = (f32[1024,1024]{1,0:T(8,128)S(1)}, f32[1024,1024]{1,0:T(8,128)}, u32[]{:S(2)}) copy-start(f32[1024,1024]{1,0:T(8,128)} %get-tuple-element.6) | copy-start | bytes 12582916
  80.6 3.4 %copy-start.4 = (f32[1024,1024]{1,0:T(8,128)S(1)}, f32[1024,1024]{1,0:T(8,128)}, u32[]{:S(2)}) copy-start(f32[1024,1024]{1,0:T(8,128)} %get-tuple-element.6) | copy-start | bytes 12582916
  92.9 3.4 %copy-start.5 = (f32[1024,1024]{1,0:T(8,128)S(1)}, f32[1024,1024]{1,0:T(8,128)}, u32[]{:S(2)}) copy-start(f32[1024,1024]{1,0:T(8,128)} %get-tuple-element.6) | copy-start | bytes 12582916
  93.0 18.3 %copy-start.9 = (f32[1024]{0:T(1024)S(1)}, f32[1024]{0:T(1024)}, u32[]{:S(2)}) copy-start(f32[1024]{0:T(1024)} %param.15) | copy-start | bytes 12292
  96.4 26.3 %copy-start.8 = (f32[1024]{0:T(1024)S(1)}, f32[1024]{0:T(1024)}, u32[]{:S(2)}) copy-start(f32[1024]{0:T(1024)} %param.14) | copy-start | bytes 12292
  172.1 11.9 %all-to-all-start.10 = ((f32[8,8,128]{2,1,0:T(8,128)}), f32[8,8,128]{2,1,0:T(8,128)S(1)}, u32[]{:S(2)}, u32[]{:S(2)}) async-start(f32[8,8,128]{2,1,0:T(8,128)} %broadcast_in_dim.51), calls=%async_computation.10 | async-start | bytes 65536 | tf_op jit(solution)/shard_map/all_to_all | solution.py:18
  176.8 75.4 %reduce-scatter.2.cloned.1.call-start = ((), (), s32[]{:S(2)}) async-start(), calls=%async_computation.15 | async-start | bytes 4718592 | tf_op jit(solution)/shard_map/reduce_scatter | solution.py:87
  184.0 12.0 %copy-start.6 = (bf16[1024,8,4,32]{0,3,2,1:T(8,128)(2,1)S(1)}, bf16[1024,8,4,32]{0,3,2,1:T(8,128)(2,1)}, u32[]{:S(2)}) copy-start(bf16[1024,8,4,32]{0,3,2,1:T(8,128)(2,1)} %copy.16) | copy-start | bytes 6291460
  194.7 1.3 copy-start.10
  201.1 15.1 %all-to-all-start.11 = ((f32[32,8,128]{2,1,0:T(8,128)}), f32[32,8,128]{2,1,0:T(8,128)S(1)}, u32[]{:S(2)}, u32[]{:S(2)}) async-start(f32[32,8,128]{2,1,0:T(8,128)} %broadcast_in_dim.53), calls=%async_computation.11 | async-start | bytes 262144 | tf_op jit(solution)/shard_map/all_to_all | solution.py:18
  216.2 53.1 %all-to-all-start.12 = ((f32[8,128,1024]{2,1,0:T(8,128)}), f32[8,128,1024]{2,1,0:T(8,128)}, u32[]{:S(2)}, u32[]{:S(2)}) async-start(f32[8,128,1024]{2,1,0:T(8,128)} %bitcast.57), calls=%async_computation.12 | async-start | bytes 8388608 | tf_op jit(solution)/shard_map/all_to_all | solution.py:93
  269.3 13.0 %all-to-all-start.13 = ((f32[4,32,1024]{2,1,0:T(8,128)}), f32[4,32,1024]{2,1,0:T(8,128)S(1)}, u32[]{:S(2)}, u32[]{:S(2)}) async-start(f32[4,32,1024]{2,1,0:T(8,128)} %bitcast.30), calls=%async_computation.14 | async-start | bytes 1048576 | tf_op jit(solution)/shard_map/all_to_all | solution.py:98
Sparse Core Ops, SparseCore 0:
  200.5 51.6 reduce-scatter.1

commit v2 on v1

v2 whole, which is shorter than its diff:
```python
import functools
import math

import jax
import jax.numpy as jnp
from jax import lax
from jax.experimental import pallas as pl
from jax.experimental.pallas import tpu as pltpu
from jax.sharding import PartitionSpec as P

K = 3


EPSILON = 0.05
PENALTY = 1.0
SCALE = 1.0 / (EPSILON * math.log(2.0))
LANES = 128
STRIP = 32
REACH = 40.0
VMEM_BYTES = 40 * 2**20
F32 = jnp.float32


def eye():
    return lax.broadcasted_iota(jnp.int32, (LANES, LANES), 0) == lax.broadcasted_iota(
        jnp.int32, (LANES, LANES), 1
    )


def to_column(row):
    return jnp.sum(jnp.where(eye(), row, 0.0), axis=1, keepdims=True)


def to_row(column):
    return jnp.sum(jnp.where(eye(), column, 0.0), axis=0, keepdims=True)


def log_combined(parts):
    top = jnp.max(parts, axis=0)
    return top + jnp.log2(jnp.sum(jnp.exp2(parts - top[None]), axis=0))


def spread(copies_ref, value):
    copies_ref[...] = jnp.broadcast_to(value[None], copies_ref.shape)


def groups_of(ref):
    return ref.shape[0]


def row_sums(base_ref, weight_ref, out_ref):
    for s in range(groups_of(out_ref)):
        held = None
        for c in range(groups_of(weight_ref)):
            tile = base_ref[s * LANES : (s + 1) * LANES, c * LANES : (c + 1) * LANES]
            term = tile * weight_ref[c : c + 1, :]
            held = term if held is None else held + term
        out_ref[s : s + 1, :] = to_row(jnp.sum(held, axis=1, keepdims=True))


def col_sums(base_ref, weight_ref, out_ref):
    held = [None] * groups_of(out_ref)
    for s in range(groups_of(weight_ref)):
        column = jnp.broadcast_to(to_column(weight_ref[s : s + 1, :]), (LANES, LANES))
        for c in range(len(held)):
            tile = base_ref[s * LANES : (s + 1) * LANES, c * LANES : (c + 1) * LANES]
            term = jnp.sum((tile * column).reshape(LANES // 8, 8, LANES), axis=0)
            held[c] = term if held[c] is None else held[c] + term
    for c, term in enumerate(held):
        out_ref[c : c + 1, :] = jnp.sum(term, axis=0, keepdims=True)


def strip_logs(scores):
    highest = jnp.max(scores, axis=1, keepdims=True)
    powers = jnp.exp2(scores - highest)
    return highest, powers, highest + jnp.log2(jnp.sum(powers, axis=1, keepdims=True))


def wide(ref):
    return jnp.concatenate([ref[c : c + 1, :] for c in range(groups_of(ref))], axis=1)


def load_rows(score_hbm, tile_ref, sem, group):
    copy = pltpu.make_async_copy(
        score_hbm.at[pl.ds(pl.multiple_of(group * LANES, LANES), LANES), :], tile_ref, sem
    )
    copy.start()
    copy.wait()


def slow_row_logs(score_hbm, tile_ref, sem, col_ref, out_ref):
    @pl.loop(0, groups_of(out_ref))
    def _(group):
        load_rows(score_hbm, tile_ref, sem, group)
        logs = []
        for q in range(LANES // STRIP):
            logs.append(strip_logs(tile_ref[q * STRIP : (q + 1) * STRIP, :] + wide(col_ref))[2])
        out_ref[pl.ds(group, 1), :] = to_row(jnp.concatenate(logs, axis=0))


def slow_col_logs(score_hbm, tile_ref, sem, row_ref, out_ref):
    count = groups_of(out_ref)
    tops = tuple(jnp.full((1, LANES), -1e30, F32) for _ in range(count))

    def highest(group, tops):
        load_rows(score_hbm, tile_ref, sem, group)
        column = to_column(row_ref[pl.ds(group, 1), :])
        return tuple(
            jnp.maximum(
                tops[c],
                jnp.max(
                    tile_ref[:, c * LANES : (c + 1) * LANES] + column, axis=0, keepdims=True
                ),
            )
            for c in range(count)
        )

    tops = lax.fori_loop(0, groups_of(row_ref), highest, tops)
    sums = tuple(jnp.zeros((1, LANES), F32) for _ in range(count))

    def summed(group, sums):
        load_rows(score_hbm, tile_ref, sem, group)
        column = to_column(row_ref[pl.ds(group, 1), :])
        return tuple(
            sums[c]
            + jnp.sum(
                jnp.exp2(tile_ref[:, c * LANES : (c + 1) * LANES] + column - tops[c]),
                axis=0,
                keepdims=True,
            )
            for c in range(count)
        )

    sums = lax.fori_loop(0, groups_of(row_ref), summed, sums)
    for c in range(count):
        out_ref[c : c + 1, :] = tops[c] + jnp.log2(sums[c])


def slow_row_weighted(score_hbm, tile_ref, sem, row_ref, col_ref, weight_ref, out_ref):
    @pl.loop(0, groups_of(out_ref))
    def _(group):
        load_rows(score_hbm, tile_ref, sem, group)
        column = to_column(row_ref[pl.ds(group, 1), :])
        sums = []
        for q in range(LANES // STRIP):
            part = slice(q * STRIP, (q + 1) * STRIP)
            plan = jnp.exp2(tile_ref[part, :] + column[part] + wide(col_ref))
            sums.append(jnp.sum(plan * wide(weight_ref), axis=1, keepdims=True))
        out_ref[pl.ds(group, 1), :] = to_row(jnp.concatenate(sums, axis=0))


def slow_col_weighted(score_hbm, tile_ref, sem, row_ref, col_ref, weight_ref, out_ref):
    count = groups_of(out_ref)
    sums = tuple(jnp.zeros((1, LANES), F32) for _ in range(count))

    def summed(group, sums):
        load_rows(score_hbm, tile_ref, sem, group)
        column = to_column(row_ref[pl.ds(group, 1), :])
        weight = to_column(weight_ref[pl.ds(group, 1), :])
        return tuple(
            sums[c]
            + jnp.sum(
                weight
                * jnp.exp2(
                    tile_ref[:, c * LANES : (c + 1) * LANES] + column + col_ref[c : c + 1, :]
                ),
                axis=0,
                keepdims=True,
            )
            for c in range(count)
        )

    sums = lax.fori_loop(0, groups_of(row_ref), summed, sums)
    for c in range(count):
        out_ref[c : c + 1, :] = sums[c]


def first_kernel(
    cost_ref, src_ref, tgt_ref, mask_ref, dual_ref, score_ref, base_ref, top_ref, copies_ref,
    allowed_ref, log_ref,
):
    classes = mask_ref.shape[0]
    mask = mask_ref[...].astype(F32).astype(jnp.bfloat16)
    ids = lax.broadcasted_iota(jnp.int32, (classes, LANES), 0)
    hot = jnp.concatenate(
        [
            jnp.where(tgt_ref[c : c + 1, :] == ids, 1.0, 0.0).astype(jnp.bfloat16)
            for c in range(groups_of(tgt_ref))
        ],
        axis=1,
    )
    allowed_of = jnp.dot(mask, hot, preferred_element_type=F32).astype(jnp.bfloat16)
    lane_ids = lax.broadcasted_iota(jnp.int32, (LANES, classes), 1).astype(F32)
    dual = wide(dual_ref) - PENALTY * SCALE
    for s in range(groups_of(log_ref)):
        label = to_column(src_ref[s : s + 1, :].astype(F32))
        src_hot = jnp.where(label == lane_ids, 1.0, 0.0).astype(jnp.bfloat16)
        allowed_ref[...] = jnp.dot(src_hot, allowed_of, preferred_element_type=F32)
        tops, logs = [], []
        for q in range(LANES // STRIP):
            rows = slice(s * LANES + q * STRIP, s * LANES + (q + 1) * STRIP)
            shifted = cost_ref[rows, :].astype(F32) - PENALTY * allowed_ref[
                q * STRIP : (q + 1) * STRIP, :
            ]
            scores = dual - shifted * SCALE
            highest, powers, log = strip_logs(scores)
            score_ref[rows, :] = scores
            base_ref[rows, :] = powers
            tops.append(highest)
            logs.append(log)
        top_ref[s : s + 1, :] = to_row(jnp.concatenate(tops, axis=0))
        log_ref[s : s + 1, :] = to_row(jnp.concatenate(logs, axis=0))
    spread(copies_ref, log_ref[...])


def rebase_kernel(
    log_target, parts_ref, score_ref, base_ref, top_ref, dual_ref, copies_ref, log_ref
):
    dual_ref[...] = log_target - log_combined(parts_ref[...])
    dual = wide(dual_ref)
    for s in range(groups_of(log_ref)):
        tops, logs = [], []
        for q in range(LANES // STRIP):
            rows = slice(s * LANES + q * STRIP, s * LANES + (q + 1) * STRIP)
            highest, powers, log = strip_logs(score_ref[rows, :] + dual)
            base_ref[rows, :] = powers
            tops.append(highest)
            logs.append(log)
        top_ref[s : s + 1, :] = to_row(jnp.concatenate(tops, axis=0))
        log_ref[s : s + 1, :] = to_row(jnp.concatenate(logs, axis=0))
    spread(copies_ref, log_ref[...])


def row_log_kernel(
    log_target, parts_ref, top_ref, base_dual_ref, base_ref, score_hbm, dual_ref, copies_ref,
    weight_ref, sum_ref, tile_ref, sem,
):
    dual_ref[...] = log_target - log_combined(parts_ref[...])
    lead = dual_ref[...] - base_dual_ref[...]
    near = jnp.max(jnp.abs(lead)) <= REACH

    @pl.when(near)
    def _():
        weight_ref[...] = jnp.exp2(lead)
        row_sums(base_ref, weight_ref, sum_ref)
        sum_ref[...] = top_ref[...] + jnp.log2(sum_ref[...])

    @pl.when(jnp.logical_not(near))
    def _():
        slow_row_logs(score_hbm, tile_ref, sem, dual_ref, sum_ref)

    spread(copies_ref, sum_ref[...])


def col_log_kernel(
    log_source, parts_ref, top_ref, base_dual_ref, base_ref, score_hbm, dual_ref, copies_ref,
    weight_ref, sum_ref, tile_ref, sem,
):
    dual_ref[...] = log_source - log_combined(parts_ref[...])
    lead = dual_ref[...] + top_ref[...]
    weight_ref[...] = jnp.exp2(jnp.minimum(lead, 100.0))
    col_sums(base_ref, weight_ref, sum_ref)
    most = jnp.max(lead)
    near = jnp.logical_and(
        most <= 60.0,
        jnp.min(jnp.log2(jnp.maximum(sum_ref[...], 1e-37))) >= jnp.maximum(most, -15.0) - 85.0,
    )

    @pl.when(near)
    def _():
        sum_ref[...] = jnp.log2(sum_ref[...]) - base_dual_ref[...]

    @pl.when(jnp.logical_not(near))
    def _():
        slow_col_logs(score_hbm, tile_ref, sem, dual_ref, sum_ref)

    spread(copies_ref, sum_ref[...])


def row_plan_kernel(
    log_target, first, parts_ref, grad_ref, dual_in_ref, row_dual_ref, top_ref, base_dual_ref,
    base_ref, score_hbm, out_ref, copies_ref, weight_ref, col_ref, sum_ref, tile_ref, sem,
):
    if first:
        dual = log_target - log_combined(parts_ref[...])
        grad = grad_ref[...]
        out_ref[...] = dual
    else:
        dual = dual_in_ref[...]
        grad = -jnp.sum(parts_ref[...], axis=0)
        out_ref[...] = grad
    lead = dual - base_dual_ref[...]
    row_lead = row_dual_ref[...] + top_ref[...]
    near = jnp.logical_and(jnp.max(jnp.abs(lead)) <= REACH, jnp.max(row_lead) <= 60.0)

    @pl.when(near)
    def _():
        weight_ref[...] = jnp.exp2(lead - log_target) * grad
        row_sums(base_ref, weight_ref, sum_ref)
        sum_ref[...] = sum_ref[...] * jnp.exp2(row_lead)

    @pl.when(jnp.logical_not(near))
    def _():
        col_ref[...] = dual - log_target
        weight_ref[...] = grad
        slow_row_weighted(score_hbm, tile_ref, sem, row_dual_ref, col_ref, weight_ref, sum_ref)

    spread(copies_ref, sum_ref[...])


def col_plan_kernel(
    log_source, parts_ref, outer_ref, dual_ref, row_dual_ref, top_ref, base_dual_ref, base_ref,
    score_hbm, out_ref, copies_ref, weight_ref, col_ref, sum_ref, tile_ref, sem,
):
    grad = outer_ref[...] - jnp.sum(parts_ref[...], axis=0)
    out_ref[...] = grad
    lead = dual_ref[...] - base_dual_ref[...]
    row_lead = row_dual_ref[...] + top_ref[...]
    near = jnp.logical_and(jnp.max(jnp.abs(lead)) <= REACH, jnp.max(row_lead) <= 60.0)

    @pl.when(near)
    def _():
        weight_ref[...] = jnp.exp2(row_lead) * grad
        col_sums(base_ref, weight_ref, sum_ref)
        sum_ref[...] = sum_ref[...] * jnp.exp2(lead - log_source)

    @pl.when(jnp.logical_not(near))
    def _():
        col_ref[...] = dual_ref[...] - log_source
        weight_ref[...] = grad
        slow_col_weighted(score_hbm, tile_ref, sem, row_dual_ref, col_ref, weight_ref, sum_ref)

    spread(copies_ref, sum_ref[...])


def grad_kernel(
    log_source, log_target,
    parts_ref, row1, row2, row3, col1, col2, col3, fbar2, fbar3, gbar1, gbar2, gbar3,
    start_top_ref, top_ref, start_base_ref, base_ref, score_hbm, out_ref,
    rows_ref, cols_ref, tile_ref, sem,
):
    fbar1 = -jnp.sum(parts_ref[...], axis=0)
    leads = [col2[...] - col1[...], col3[...] - col1[...]]
    row_leads = [ref[...] + top_ref[...] for ref in (row1, row2, row3)]
    near = jnp.logical_and(
        jnp.maximum(jnp.max(jnp.abs(leads[0])), jnp.max(jnp.abs(leads[1]))) <= REACH,
        jnp.max(row_leads[2]) <= 60.0,
    )
    count = groups_of(col1)

    @pl.when(near)
    def _():
        rows_ref[0] = -jnp.exp2(row1[...] + start_top_ref[...] - log_source) * fbar1
        rows_ref[1] = -jnp.exp2(row_leads[0])
        rows_ref[2] = -jnp.exp2(row_leads[1])
        rows_ref[3] = -jnp.exp2(row_leads[2])
        rows_ref[4] = rows_ref[2] * fbar2[...]
        rows_ref[5] = rows_ref[3] * fbar3[...]
        cols_ref[1] = jnp.exp2(jnp.full_like(leads[0], -log_target)) * gbar1[...]
        cols_ref[2] = jnp.exp2(leads[0] - log_target) * gbar2[...]
        cols_ref[3] = jnp.exp2(leads[1] - log_target) * gbar3[...]
        cols_ref[4] = jnp.exp2(jnp.full_like(leads[0], -log_source))
        cols_ref[5] = jnp.exp2(leads[0] - log_source)
        for s in range(groups_of(row1)):
            columns = [to_column(rows_ref[k, s : s + 1, :]) for k in range(6)]
            for q in range(LANES // STRIP):
                rows = slice(s * LANES + q * STRIP, s * LANES + (q + 1) * STRIP)
                strips = [
                    jnp.broadcast_to(part[q * STRIP : (q + 1) * STRIP], (STRIP, LANES))
                    for part in columns
                ]
                for c in range(count):
                    lanes = slice(c * LANES, (c + 1) * LANES)
                    weight = strips[1] * cols_ref[1, c : c + 1, :]
                    for k in range(2, 6):
                        weight = weight + strips[k] * cols_ref[k, c : c + 1, :]
                    value = base_ref[rows, lanes] * weight + start_base_ref[rows, lanes] * strips[0]
                    out_ref[rows, lanes] = value.astype(jnp.bfloat16)

    @pl.when(jnp.logical_not(near))
    def _():
        zero = jnp.zeros_like(fbar1)
        for k, (row, value) in enumerate(((row1, fbar1), (row2, fbar2[...]), (row3, fbar3[...]))):
            rows_ref[k] = row[...]
            rows_ref[3 + k] = value
        for k, (col, value) in enumerate(
            ((zero, None), (col1[...], gbar1), (col2[...], gbar2), (col3[...], gbar3))
        ):
            cols_ref[k] = col
            if value is not None:
                cols_ref[3 + k] = value[...]

        @pl.loop(0, groups_of(row1))
        def _(group):
            load_rows(score_hbm, tile_ref, sem, group)
            columns = [to_column(rows_ref[k, pl.ds(group, 1), :]) for k in range(6)]
            for c in range(count):
                lanes = slice(c * LANES, (c + 1) * LANES)
                value = jnp.zeros((LANES, LANES), F32)
                for k in reversed(range(3)):
                    scores = tile_ref[:, lanes] + columns[k]
                    plan_q = jnp.exp2(scores + (cols_ref[k + 1, c : c + 1, :] - log_target))
                    plan_r = jnp.exp2(scores + (cols_ref[k, c : c + 1, :] - log_source))
                    value = value + plan_q * cols_ref[4 + k, c : c + 1, :]
                    value = value + plan_r * columns[3 + k]
                start = pl.multiple_of(group * LANES, LANES)
                out_ref[pl.ds(start, LANES), lanes] = (-value).astype(jnp.bfloat16)


def call(kernel, arguments, outs, scratch=(), in_hbm=(), flops=0, name=None):
    specs = [
        pl.BlockSpec(memory_space=pl.ANY if at in in_hbm else pltpu.VMEM)
        for at in range(len(arguments))
    ]
    return pl.pallas_call(
        kernel,
        out_shape=outs,
        in_specs=specs,
        out_specs=[pl.BlockSpec(memory_space=pltpu.VMEM)] * len(outs),
        scratch_shapes=list(scratch),
        compiler_params=pltpu.CompilerParams(vmem_limit_bytes=VMEM_BYTES),
        name=name,
    )(*arguments)


def exchanged(copies, axis):
    return lax.all_to_all(copies, axis, 0, 0, tiled=True)


def body(cost, src_label, tgt_label, class_mask, g_start, f_bar, g_bar, src_emb, tgt_emb):
    row_count = lax.axis_size("rows")
    col_count = lax.axis_size("cols")
    src_rows, tgt_cols = cost.shape
    width = src_emb.shape[1]
    log_source = -math.log2(src_rows * row_count)
    log_target = -math.log2(tgt_cols * col_count)
    row_shape = (src_rows // LANES, LANES)
    col_shape = (tgt_cols // LANES, LANES)
    src_label, f_bar = src_label.reshape(row_shape), f_bar.reshape(row_shape)
    tgt_label, g_bar = tgt_label.reshape(col_shape), g_bar.reshape(col_shape)
    g_start = (g_start * SCALE).reshape(col_shape)

    def array(shape, dtype=F32):
        return jax.ShapeDtypeStruct(shape, dtype)

    matrix = array(cost.shape)
    row_vector, col_vector = array(row_shape), array(col_shape)
    row_copies = array((col_count,) + row_shape)
    col_copies = array((row_count,) + col_shape)
    row_held, col_held = pltpu.VMEM(row_shape, F32), pltpu.VMEM(col_shape, F32)
    slow = [pltpu.VMEM((LANES, tgt_cols), F32), pltpu.SemaphoreType.DMA]

    score, start_base, start_top, copies = call(
        first_kernel,
        (cost, src_label, tgt_label, class_mask, g_start),
        [matrix, matrix, row_vector, row_copies],
        [pltpu.VMEM((LANES, tgt_cols), F32), row_held],
        name="first_row_logs",
    )

    def col_logs(parts, top, base_dual, base):
        return call(
            functools.partial(col_log_kernel, log_source),
            (parts, top, base_dual, base, score),
            [row_vector, col_copies],
            [row_held, col_held] + slow,
            in_hbm=(4,),
            name="col_logs",
        )

    zero = jnp.zeros(col_shape, F32)
    row1, copies = col_logs(exchanged(copies, "cols"), start_top, zero, start_base)
    base, top, col1, copies = call(
        functools.partial(rebase_kernel, log_target),
        (exchanged(copies, "rows"), score),
        [matrix, row_vector, col_vector, row_copies],
        [row_held],
        name="second_row_logs",
    )
    row2, copies = col_logs(exchanged(copies, "cols"), top, col1, base)
    col2, copies = call(
        functools.partial(row_log_kernel, log_target),
        (exchanged(copies, "rows"), top, col1, base, score),
        [col_vector, row_copies],
        [col_held, row_held] + slow,
        in_hbm=(4,),
        name="third_row_logs",
    )
    row3, copies = col_logs(exchanged(copies, "cols"), top, col1, base)

    def row_plan(first, parts, grad, dual, row):
        return call(
            functools.partial(row_plan_kernel, log_target, first),
            (parts, grad, dual, row, top, col1, base, score),
            [col_vector, row_copies],
            [col_held, col_held, row_held] + slow,
            in_hbm=(7,),
            name="row_plan",
        )

    def col_plan(parts, outer, dual, row, top, base_dual, base):
        return call(
            functools.partial(col_plan_kernel, log_source),
            (parts, outer, dual, row, top, base_dual, base, score),
            [row_vector, col_copies],
            [row_held, col_held, col_held] + slow,
            in_hbm=(7,),
            name="col_plan",
        )

    none = jnp.zeros(row_shape, F32)
    col3, copies = row_plan(True, exchanged(copies, "rows"), g_bar, col2, row3)
    fbar3, copies = col_plan(exchanged(copies, "cols"), f_bar, col2, row3, top, col1, base)
    gbar2, copies = row_plan(False, exchanged(copies, "rows"), g_bar, col2, row2)
    fbar2, copies = col_plan(exchanged(copies, "cols"), none, col1, row2, top, col1, base)
    gbar1, copies = row_plan(False, exchanged(copies, "rows"), g_bar, col1, row1)
    parts = exchanged(copies, "cols")
    (rounded,) = call(
        functools.partial(grad_kernel, log_source, log_target),
        (
            parts, row1, row2, row3, col1, col2, col3, fbar2, fbar3, gbar1, gbar2, g_bar,
            start_top, top, start_base, base, score,
        ),
        [array(cost.shape, jnp.bfloat16)],
        [pltpu.VMEM((6,) + row_shape, F32), pltpu.VMEM((7,) + col_shape, F32)] + slow,
        in_hbm=(16,),
        name="cost_grad",
    )
    x_count, z_count = 4, row_count // 4
    owned = width // row_count
    src_ordered = src_emb.reshape(src_rows, x_count, z_count, owned).transpose(0, 2, 1, 3)
    along_z = [[x * z_count + z for z in range(z_count)] for x in range(x_count)]
    along_x = [[x * z_count + z for x in range(x_count)] for z in range(z_count)]
    y_part = lax.dot_general(
        src_ordered.reshape(src_rows, width),
        rounded,
        (((0,), (0,)), ((), ())),
        preferred_element_type=F32,
    )
    y_part = lax.psum_scatter(
        y_part, "rows", scatter_dimension=0, tiled=True, axis_index_groups=along_z
    )
    x_part = lax.dot_general(
        tgt_emb, rounded, (((0,), (1,)), ((), ())), preferred_element_type=F32
    )
    x_blocks = lax.all_to_all(
        x_part.reshape(col_count, width // col_count, src_rows), "cols", 0, 0, tiled=True
    )
    grad_x = jnp.sum(x_blocks, axis=0)
    fbar1, copies = col_plan(parts, none, zero, row1, start_top, zero, start_base)
    g_start_bar = -jnp.sum(exchanged(copies, "rows"), axis=0).reshape(tgt_cols)
    y_blocks = lax.all_to_all(
        y_part.reshape(x_count, owned, tgt_cols), "rows", 0, 0, tiled=True, axis_index_groups=along_x
    )
    grad_y = jnp.sum(y_blocks, axis=0)
    return (g_start_bar, grad_x, grad_y)


def solution(mesh):
    placed = (
        P("rows", "cols"),
        P("rows"),
        P("cols"),
        P(),
        P("cols"),
        P("rows"),
        P("cols"),
        P("rows", None),
        P("cols", None),
    )
    return jax.shard_map(
        body,
        mesh=mesh,
        in_specs=placed,
        out_specs=(P("cols"), P("cols", "rows"), P("rows", "cols")),
        check_vma=False,
    )
```

time: 292 us -> 268 us (0.918)
  other arithmetic: 54.6 us -> 5.56 us
  Pallas kernels: 0 us -> 24.9 us
  local copies, waits for them, and re-layouts: 14.8 us -> 21.7 us
  matrix products: 15.4 us -> 11.9 us
    pallas_call x0 -> x13, Pallas kernels: none -> 24.9 us  [call(): pl.pallas_call(kernel, out_shape=outs, in_specs=specs, out_specs=[pl.Bloc...]
    reduce_sum x23 -> x1, other arithmetic: 24.9 us -> 0.04 us  [body(): g_start_bar = -jnp.sum(exchanged(copies, 'rows'), axis=0).reshape(tgt_cols)]
    reduce_max x11 -> x0, other arithmetic: 14.2 us -> none  [the longest x5 14.1 us: log_total(): highest = jnp.max(scores, axis=reduced, keepdims=True)]
    convert_element_type x1 -> x0, other arithmetic: 10.7 us -> none  [body(): rounded = cost_grad.astype(jnp.bfloat16)]
    unnamed x23 -> x31, local copies, waits for them, and re-layouts: 8.17 us -> 16.5 us
    dot_general x1 -> x0, matrix products: 5.08 us -> none  [body(): lax.dot_general(src_allowed, tgt_hot, (((1,), (1,)), ((), ())), preferred...]
    reduce_scatter x1, waiting for transfers between devices: 31.3 us -> 27.5 us  [body(): lax.psum_scatter(y_part, 'rows', scatter_dimension=0, tiled=True, axis_in...]
    all_to_all x1, waiting for transfers between devices: 15 us -> 18.7 us  [body(): lax.all_to_all(x_part.reshape(col_count, width // col_count, src_rows), '...]
where the time goes in v2:
time: 268 us
  blocking collectives  115 us (43%)
  waiting for transfers between devices  57.5 us (21%)
  Pallas kernels  24.9 us (9%)
  local copies, waits for them, and re-layouts  21.7 us (8%)
  starting transfers between devices  16.9 us (6%)
  between operations  14.2 us (5%)
  matrix products  11.9 us (4%)
  other arithmetic  5.56 us (2%)
    all_to_all x10, blocking collectives, exchanged(): return lax.all_to_all(copies, axis, 0, 0, tiled=True)  115 us
    reduce_scatter x1, waiting for transfers between devices, body(): lax.psum_scatter(y_part, 'rows', scatter_dimension=0, tiled=True, axis_in...  27.5 us
    pallas_call x13, Pallas kernels, call(): pl.pallas_call(kernel, out_shape=outs, in_specs=specs, out_specs=[pl.Bloc...  24.9 us
    all_to_all x1, waiting for transfers between devices, body(): lax.all_to_all(x_part.reshape(col_count, width // col_count, src_rows), '...  18.7 us
    unnamed x31, local copies, waits for them, and re-layouts  16.5 us
    all_to_all x2, starting transfers between devices, exchanged(): return lax.all_to_all(copies, axis, 0, 0, tiled=True)  8.59 us
    dot_general x1, matrix products, body(): lax.dot_general(src_ordered.reshape(src_rows, width), rounded, (((0,), (0...  5.96 us
    dot_general x1, matrix products, body(): lax.dot_general(tgt_emb, rounded, (((0,), (1,)), ((), ())), preferred_ele...  5.92 us
  transfers between devices with their start and end apart: 5, of which 4 were waited for; matrix products, arithmetic and copies ran while one was open for 7% of the time, Pallas kernels for 0%

profile of v2, /device:TPU:8, one launch (start us, length us, event | category | flops | bytes accessed | tf_op | source)
XLA Modules:
  0.0 267.9 jit_solution(17196188446533128308)
XLA Ops:
  7.2 0.0 copy-start
  7.2 0.8 multiply_bitcast_fusion.dual_ref
  8.0 0.0 copy-start.8
  8.0 1.6 copy-done.8
  9.6 0.8 copy-done.10
  10.4 0.7 copy-done.11
  11.1 0.7 copy-done.12
  11.7 2.7 %first_row_logs.1 = (f32[1024,1024]{1,0:T(8,128)S(1)}, f32[1024,1024]{1,0:T(8,128)S(1)}, f32[8,128]{1,0:T(8,128)S(1)}, f32[8,8,128]{2,1,0:T(8,128)S(1)}) custom-call(bf16[1024,1024]{1,0:T(8,128)(2,1)S(1)} %copy-done.8, s32[8,128]{1,0:T(8,128)S(1)} %bitcast.26, s32[8,128]{1,0:T(8,128)S(1)} %bitcast.27, s32[64,64]{1,0:T(8,128)S(1)} %copy-done.10, ...), custom_call_target="tpu_custom_call" | custom-call | tf_op jit(solution)/shard_map/first_row_logs/pallas_call | solution.py:415
  14.4 0.0 copy-start.5
  14.4 0.0 copy-start.1
  14.5 8.7 %all_to_all.70.parts_ref = f32[8,8,128]{2,1,0:T(8,128)S(1)} all-to-all(f32[8,8,128]{2,1,0:T(8,128)S(1)} %get-tuple-element.30), channel_id=1, replica_groups=mesh['rows'=32,'cols'=8] {'cols'}, dimensions={0} | all-to-all | bytes 65536 | tf_op jit(solution)/shard_map/all_to_all | solution.py:427
  23.2 3.5 %col_logs.3 = (f32[8,128]{1,0:T(8,128)S(1)}, f32[32,8,128]{2,1,0:T(8,128)S(1)}) custom-call(f32[8,8,128]{2,1,0:T(8,128)S(1)} %all_to_all.70.parts_ref, f32[8,128]{1,0:T(8,128)S(1)} %get-tuple-element.31.top_ref.start_top_ref, f32[8,128]{1,0:T(8,128)S(1)} %broadcast_1_base_dual_ref_outer_ref_dual_ref.2.base_dual_ref.outer_ref.dual_ref, ...), custom_call_target="tpu_custom_call" | custom-call | tf_op jit(solution)/shard_map/col_logs/pallas_call | solution.py:415
  26.6 0.0 copy-done.5
  26.7 21.4 %all_to_all.71.parts_ref = f32[32,8,128]{2,1,0:T(8,128)S(1)} all-to-all(f32[32,8,128]{2,1,0:T(8,128)S(1)} %get-tuple-element.34), channel_id=1, replica_groups=mesh['rows'=32,'cols'=8] {'rows'}, dimensions={0} | all-to-all | bytes 262144 | tf_op jit(solution)/shard_map/all_to_all | solution.py:427
  48.1 2.5 second_row_logs.1
  50.5 0.0 copy-start.3
  50.5 7.8 %all_to_all.72.parts_ref = f32[8,8,128]{2,1,0:T(8,128)S(1)} all-to-all(f32[8,8,128]{2,1,0:T(8,128)S(1)} %get-tuple-element.35), channel_id=1, replica_groups=mesh['rows'=32,'cols'=8] {'cols'}, dimensions={0} | all-to-all | bytes 65536 | tf_op jit(solution)/shard_map/all_to_all | solution.py:427
  58.3 3.4 %col_logs.4 = (f32[8,128]{1,0:T(8,128)S(1)}, f32[32,8,128]{2,1,0:T(8,128)S(1)}) custom-call(f32[8,8,128]{2,1,0:T(8,128)S(1)} %all_to_all.72.parts_ref, f32[8,128]{1,0:T(8,128)S(1)} %get-tuple-element.36.top_ref, f32[8,128]{1,0:T(8,128)S(1)} %get-tuple-element.37.base_dual_ref.dual_ref.dual_in_ref.col1, f32[1024,1024]{1,0:T(8,128)S(1)} %get-tuple-element.38.base_ref, ...), custom_call_target="tpu_custom_call" | custom-call | tf_op jit(solution)/shard_map/col_logs/pallas_call | solution.py:415
  61.8 13.8 %all_to_all.73.parts_ref = f32[32,8,128]{2,1,0:T(8,128)S(1)} all-to-all(f32[32,8,128]{2,1,0:T(8,128)S(1)} %get-tuple-element.39), channel_id=1, replica_groups=mesh['rows'=32,'cols'=8] {'rows'}, dimensions={0} | all-to-all | bytes 262144 | tf_op jit(solution)/shard_map/all_to_all | solution.py:427
  75.6 0.6 third_row_logs.1
  76.2 7.1 %all_to_all.74.parts_ref = f32[8,8,128]{2,1,0:T(8,128)S(1)} all-to-all(f32[8,8,128]{2,1,0:T(8,128)S(1)} %get-tuple-element.40), channel_id=1, replica_groups=mesh['rows'=32,'cols'=8] {'cols'}, dimensions={0} | all-to-all | bytes 65536 | tf_op jit(solution)/shard_map/all_to_all | solution.py:427
  83.3 3.4 %col_logs.5 = (f32[8,128]{1,0:T(8,128)S(1)}, f32[32,8,128]{2,1,0:T(8,128)S(1)}) custom-call(f32[8,8,128]{2,1,0:T(8,128)S(1)} %all_to_all.74.parts_ref, f32[8,128]{1,0:T(8,128)S(1)} %get-tuple-element.36.top_ref, f32[8,128]{1,0:T(8,128)S(1)} %get-tuple-element.37.base_dual_ref.dual_ref.dual_in_ref.col1, f32[1024,1024]{1,0:T(8,128)S(1)} %get-tuple-element.38.base_ref, ...), custom_call_target="tpu_custom_call" | custom-call | tf_op jit(solution)/shard_map/col_logs/pallas_call | solution.py:415
  86.7 13.8 %all_to_all.75.parts_ref = f32[32,8,128]{2,1,0:T(8,128)S(1)} all-to-all(f32[32,8,128]{2,1,0:T(8,128)S(1)} %get-tuple-element.41), channel_id=1, replica_groups=mesh['rows'=32,'cols'=8] {'rows'}, dimensions={0} | all-to-all | bytes 262144 | tf_op jit(solution)/shard_map/all_to_all | solution.py:427
  100.5 0.0 copy-done.9
  100.5 0.6 row_plan.3
  101.1 7.1 %all_to_all.76.parts_ref = f32[8,8,128]{2,1,0:T(8,128)S(1)} all-to-all(f32[8,8,128]{2,1,0:T(8,128)S(1)} %get-tuple-element.44), channel_id=1, replica_groups=mesh['rows'=32,'cols'=8] {'cols'}, dimensions={0} | all-to-all | bytes 65536 | tf_op jit(solution)/shard_map/all_to_all | solution.py:427
  108.2 0.0 copy-done.13
  108.2 0.5 col_plan.3
  108.7 13.8 %all_to_all.77.parts_ref = f32[32,8,128]{2,1,0:T(8,128)S(1)} all-to-all(f32[32,8,128]{2,1,0:T(8,128)S(1)} %get-tuple-element.45), channel_id=1, replica_groups=mesh['rows'=32,'cols'=8] {'rows'}, dimensions={0} | all-to-all | bytes 262144 | tf_op jit(solution)/shard_map/all_to_all | solution.py:427
  122.6 0.5 row_plan.4
  123.1 7.8 %all_to_all.78.parts_ref = f32[8,8,128]{2,1,0:T(8,128)S(1)} all-to-all(f32[8,8,128]{2,1,0:T(8,128)S(1)} %get-tuple-element.47), channel_id=1, replica_groups=mesh['rows'=32,'cols'=8] {'cols'}, dimensions={0} | all-to-all | bytes 65536 | tf_op jit(solution)/shard_map/all_to_all | solution.py:427
  130.9 0.5 col_plan.4
  131.5 13.9 %all_to_all.79.parts_ref = f32[32,8,128]{2,1,0:T(8,128)S(1)} all-to-all(f32[32,8,128]{2,1,0:T(8,128)S(1)} %get-tuple-element.48), channel_id=1, replica_groups=mesh['rows'=32,'cols'=8] {'rows'}, dimensions={0} | all-to-all | bytes 262144 | tf_op jit(solution)/shard_map/all_to_all | solution.py:427
  145.3 0.0 copy-done.1
  145.3 0.0 copy-done.3
  145.3 1.3 row_plan.5
  146.6 4.7 %all-to-all-start.10 = ((f32[8,8,128]{2,1,0:T(8,128)}), f32[8,8,128]{2,1,0:T(8,128)S(1)}, u32[]{:S(2)}, u32[]{:S(2)}) async-start(f32[8,8,128]{2,1,0:T(8,128)} %get-tuple-element.50), calls=%async_computation.10 | async-start | bytes 65536 | tf_op jit(solution)/shard_map/all_to_all | solution.py:427
  151.4 0.0 reduce-scatter.2.cloned.1.call-start
  151.4 4.0 %copy.12 = bf16[1024,1024]{0,1:T(8,128)(2,1)} copy(bf16[1024,1024]{1,0:T(8,128)(2,1)} %param.16) | data formatting | bytes 4194304 | tf_op args[7]
  155.3 3.2 %copy.13 = bf16[1024,8,4,32]{0,3,2,1:T(8,128)(2,1)} copy(bf16[1024,8,4,32]{0,3,1,2:T(8,128)(2,1)} %bitcast.29) | data formatting | bytes 4194304 | tf_op jit(solution)/shard_map/transpose | solution.py:531
  158.5 0.0 all-to-all-done.10.parts_ref
  158.5 2.2 copy-done.4
  160.7 2.2 copy-done.6
  162.9 4.2 %cost_grad.1 = bf16[1024,1024]{1,0:T(8,128)(2,1)} custom-call(f32[8,8,128]{2,1,0:T(8,128)S(1)} %all-to-all-done.10.parts_ref, f32[8,128]{1,0:T(8,128)S(1)} %get-tuple-element.49.row_dual_ref.row1, f32[8,128]{1,0:T(8,128)S(1)} %get-tuple-element.46.row_dual_ref.row2, f32[8,128]{1,0:T(8,128)S(1)} %get-tuple-element.43.row_dual_ref.row3, ...), custom_call_target="tpu_custom_call" | custom-call | tf_op jit(solution)/shard_map/cost_grad/pallas_call | solution.py:415
  167.1 0.0 copy-done.14
  167.1 6.0 %convolution_bitcast_fusion = f32[1024,1024]{0,1:T(8,128)} fusion(bf16[1024,1024]{1,0:T(8,128)(2,1)} %cost_grad.1, bf16[1024,1024]{0,1:T(8,128)(2,1)S(1)} %bitcast.31), kind=kOutput, calls=%fused_computation | convolution fusion | flops 2147483648 | bytes 8388608 | tf_op jit(solution)/shard_map/dot_general | solution.py:534
  173.0 0.0 reduce-scatter.2.cloned.1.call-update
  173.1 0.0 copy-start.2
  173.1 2.2 copy-done.2
  175.3 2.2 copy-done.7
  177.4 1.2 col_plan.5
  178.6 3.9 %all-to-all-start.11 = ((f32[32,8,128]{2,1,0:T(8,128)}), f32[32,8,128]{2,1,0:T(8,128)S(1)}, u32[]{:S(2)}, u32[]{:S(2)}) async-start(f32[32,8,128]{2,1,0:T(8,128)} %get-tuple-element.51), calls=%async_computation.11 | async-start | bytes 262144 | tf_op jit(solution)/shard_map/all_to_all | solution.py:427
  182.5 0.0 copy-done
  182.5 5.9 %fusion = f32[1024,1024]{0,1:T(8,128)} fusion(bf16[1024,1024]{1,0:T(8,128)(2,1)} %cost_grad.1, bf16[1024,1024]{1,0:T(8,128)(2,1)S(1)} %copy-done), kind=kOutput, calls=%fused_computation.3 | convolution fusion | flops 2147483648 | bytes 8388608 | tf_op jit(solution)/shard_map/dot_general | solution.py:543
  188.4 5.8 %all-to-all-done.11 = f32[32,8,128]{2,1,0:T(8,128)S(1)} async-done(((f32[32,8,128]{2,1,0:T(8,128)}), f32[32,8,128]{2,1,0:T(8,128)S(1)}, u32[]{:S(2)}, u32[]{:S(2)}) %all-to-all-start.11) | async-done | bytes 131104 | tf_op jit(solution)/shard_map/all_to_all | solution.py:427
  194.2 4.8 %all-to-all-start.12 = ((f32[8,128,1024]{2,1,0:T(8,128)}), f32[8,128,1024]{2,1,0:T(8,128)}, u32[]{:S(2)}, u32[]{:S(2)}) async-start(f32[8,128,1024]{2,1,0:T(8,128)} %bitcast.30), calls=%async_computation.12 | async-start | bytes 8388608 | tf_op jit(solution)/shard_map/all_to_all | solution.py:546
  199.1 27.5 %reduce-scatter.2.cloned.1.call-done = f32[128,1024]{0,1:T(8,128)} async-done(((f32[1024,1024]{0,1:T(8,128)}), f32[128,1024]{0,1:T(8,128)}) %reduce-scatter.2.cloned.1.call-update) | async-done | bytes 524304 | tf_op jit(solution)/shard_map/reduce_scatter | solution.py:540
  226.6 2.1 copy.14
  228.7 18.7 %all-to-all-done.12 = f32[8,128,1024]{2,1,0:T(8,128)} async-done(((f32[8,128,1024]{2,1,0:T(8,128)}), f32[8,128,1024]{2,1,0:T(8,128)}, u32[]{:S(2)}, u32[]{:S(2)}) %all-to-all-start.12) | async-done | bytes 4194336 | tf_op jit(solution)/shard_map/all_to_all | solution.py:546
  247.4 3.5 %all-to-all-start.13 = ((f32[4,32,1024]{2,1,0:T(8,128)}), f32[4,32,1024]{2,1,0:T(8,128)S(1)}, u32[]{:S(2)}, u32[]{:S(2)}) async-start(f32[4,32,1024]{2,1,0:T(8,128)} %bitcast.12), calls=%async_computation.14 | async-start | bytes 1048576 | tf_op jit(solution)/shard_map/all_to_all | solution.py:552
  250.9 0.6 negate_bitcast_fusion
  251.5 3.4 %reduce_sum.28 = f32[128,1024]{1,0:T(8,128)} reduce(f32[8,128,1024]{2,1,0:T(8,128)} %all-to-all-done.12, f32[]{:T(128)} %constant.0.clone.1), dimensions={0}, to_apply=%region_1.0 | reduce | flops 917504 | bytes 4718596 | tf_op jit(solution)/shard_map/reduce_sum | solution.py:549
  254.9 5.5 %all-to-all-done.13 = f32[4,32,1024]{2,1,0:T(8,128)S(1)} async-done(((f32[4,32,1024]{2,1,0:T(8,128)}), f32[4,32,1024]{2,1,0:T(8,128)S(1)}, u32[]{:S(2)}, u32[]{:S(2)}) %all-to-all-start.13) | async-done | bytes 524320 | tf_op jit(solution)/shard_map/all_to_all | solution.py:552
  260.4 0.7 reduce_sum.29
  (11 shorter events, 0.1 us)
Async XLA Ops:
  7.2 175.4 %copy-start = (bf16[1024,1024]{1,0:T(8,128)(2,1)S(1)}, bf16[1024,1024]{1,0:T(8,128)(2,1)}, u32[]{:S(2)}) copy-start(bf16[1024,1024]{1,0:T(8,128)(2,1)} %param.17) | copy-start | bytes 6291460
  8.0 1.6 copy-start.8
  9.6 0.8 copy-start.10
  10.4 0.7 copy-start.11
  11.1 0.7 copy-start.12
  14.4 12.2 %copy-start.5 = (f32[1024,1024]{1,0:T(8,128)}, f32[1024,1024]{1,0:T(8,128)S(1)}, u32[]{:S(2)}) copy-start(f32[1024,1024]{1,0:T(8,128)S(1)} %get-tuple-element.32.base_ref.start_base_ref) | copy-start | bytes 12582916
  14.4 130.9 %copy-start.1 = (f32[1024,1024]{1,0:T(8,128)}, f32[1024,1024]{1,0:T(8,128)S(1)}, u32[]{:S(2)}) copy-start(f32[1024,1024]{1,0:T(8,128)S(1)} %get-tuple-element.33.score_hbm.score_ref) | copy-start | bytes 12582916
  50.5 94.8 %copy-start.3 = (f32[1024,1024]{1,0:T(8,128)}, f32[1024,1024]{1,0:T(8,128)S(1)}, u32[]{:S(2)}) copy-start(f32[1024,1024]{1,0:T(8,128)S(1)} %get-tuple-element.38.base_ref) | copy-start | bytes 12582916
  83.3 17.2 %copy-start.9 = (f32[1024]{0:T(1024)S(1)}, f32[1024]{0:T(1024)}, u32[]{:S(2)}) copy-start(f32[1024]{0:T(1024)} %param.15) | copy-start | bytes 12292
  100.5 7.7 %copy-start.13 = (f32[1024]{0:T(1024)S(1)}, f32[1024]{0:T(1024)}, u32[]{:S(2)}) copy-start(f32[1024]{0:T(1024)} %param.14) | copy-start | bytes 12292
  146.6 11.9 %all-to-all-start.10 = ((f32[8,8,128]{2,1,0:T(8,128)}), f32[8,8,128]{2,1,0:T(8,128)S(1)}, u32[]{:S(2)}, u32[]{:S(2)}) async-start(f32[8,8,128]{2,1,0:T(8,128)} %get-tuple-element.50), calls=%async_computation.10 | async-start | bytes 65536 | tf_op jit(solution)/shard_map/all_to_all | solution.py:427
  151.4 75.2 %reduce-scatter.2.cloned.1.call-start = ((), (), s32[]{:S(2)}) async-start(), calls=%async_computation.15 | async-start | bytes 4718592 | tf_op jit(solution)/shard_map/reduce_scatter | solution.py:540
  158.5 2.2 copy-start.4
  160.7 2.2 copy-start.6
  162.9 4.2 %copy-start.14 = (bf16[1024,8,4,32]{0,3,2,1:T(8,128)(2,1)S(1)}, bf16[1024,8,4,32]{0,3,2,1:T(8,128)(2,1)}, u32[]{:S(2)}) copy-start(bf16[1024,8,4,32]{0,3,2,1:T(8,128)(2,1)} %copy.13) | copy-start | bytes 6291460
  173.1 2.2 copy-start.2
  175.3 2.2 copy-start.7
  178.6 15.6 %all-to-all-start.11 = ((f32[32,8,128]{2,1,0:T(8,128)}), f32[32,8,128]{2,1,0:T(8,128)S(1)}, u32[]{:S(2)}, u32[]{:S(2)}) async-start(f32[32,8,128]{2,1,0:T(8,128)} %get-tuple-element.51), calls=%async_computation.11 | async-start | bytes 262144 | tf_op jit(solution)/shard_map/all_to_all | solution.py:427
  194.2 53.1 %all-to-all-start.12 = ((f32[8,128,1024]{2,1,0:T(8,128)}), f32[8,128,1024]{2,1,0:T(8,128)}, u32[]{:S(2)}, u32[]{:S(2)}) async-start(f32[8,128,1024]{2,1,0:T(8,128)} %bitcast.30), calls=%async_computation.12 | async-start | bytes 8388608 | tf_op jit(solution)/shard_map/all_to_all | solution.py:546
  247.4 13.0 %all-to-all-start.13 = ((f32[4,32,1024]{2,1,0:T(8,128)}), f32[4,32,1024]{2,1,0:T(8,128)S(1)}, u32[]{:S(2)}, u32[]{:S(2)}) async-start(f32[4,32,1024]{2,1,0:T(8,128)} %bitcast.12), calls=%async_computation.14 | async-start | bytes 1048576 | tf_op jit(solution)/shard_map/all_to_all | solution.py:552
Sparse Core Ops, SparseCore 0:
  173.2 53.3 reduce-scatter.1
